TPU v7x, 512 devices: a whole 4x4x16 slice. The times are simulated.
512 devices in a mesh: vocab: 64 (over z, y), tok: 8 (over x, core).
Axes of the slice: x: 4, y: 4, z: 16, core: 2. Of those that a mesh axis runs over, the one named last changes fastest.
Arguments:
- hidden: bfloat16 [1024, 3584], P('tok', 'vocab'), may hold values from -8 to 8
- head_weight: bfloat16 [3584, 81920], P('tok', 'vocab'), may hold values from -4 to 4
- targets: int32 [1024], P('tok'), may hold values from 0 to 81919
- response_mask: int32 [1024], P('tok'), may hold values 0 or 1
- labels: int32 [8], P('tok'), may hold values 0 or 1
- reference_sums: float32 [8, 2], P('tok'), may hold values from -48 to 48
Outputs:
- mean_loss: float32 [], replicated
- margins: float32 [8], P('tok')
- hidden_grad: bfloat16 [1024, 3584], P('tok', 'vocab')
- head_grad: bfloat16 [3584, 81920], P('tok', 'vocab')
All inputs are finite; a program needn't handle non-finite values. No bound on the sum of `response_mask` or of `labels` on one device may be relied on, other than what follows from the above.
Results may differ from a plain program's by a relative error of at most 0.0085.
Values may be sent and summed in bfloat16 or wider, within the bound.
A program may use at most 64 MiB of HBM per device.

v0:
```python
import math

import jax
import jax.numpy as jnp
from jax import lax
from jax.sharding import PartitionSpec as P

beta_scale = 0.1
tie_offset = math.log(2.0)
tie_const = math.log(3.0)
grad_scale = 512.0


def pair_terms(margins, labels):
    winner = labels.astype(jnp.float32)
    log_tie = (
        tie_const
        + margins
        - tie_offset
        - jax.nn.softplus(margins - tie_offset)
        - jax.nn.softplus(margins + tie_offset)
    )
    losses = winner * jax.nn.softplus(tie_offset - margins) - (1.0 - winner) * log_tie
    slopes = -winner * jax.nn.sigmoid(tie_offset - margins) - (1.0 - winner) * (
        1.0 - jax.nn.sigmoid(margins - tie_offset) - jax.nn.sigmoid(margins + tie_offset)
    )
    return (losses, slopes)


def local(hidden, head_weight, targets, response_mask, labels, reference_sums):
    tok_rows = hidden.shape[0]
    vocab_cols = head_weight.shape[1]
    tok_count = lax.axis_size("tok")
    pair_local = labels.shape[0]
    pair_total = pair_local * tok_count
    span = tok_rows // (2 * pair_local)
    rows_full = lax.all_gather(hidden, "vocab", axis=1, tiled=True)
    token_cols = lax.all_to_all(rows_full, "tok", split_axis=1, concat_axis=0, tiled=True)
    head_full = lax.all_gather(head_weight, "tok", axis=0, tiled=True)
    logits = jnp.dot(rows_full, head_full, preferred_element_type=jnp.float32)
    offset = lax.axis_index("vocab") * vocab_cols
    columns = lax.broadcasted_iota(jnp.int32, (1, vocab_cols), 1) + offset
    matched = columns == targets[:, None]
    local_max = jnp.max(logits, axis=1)
    local_target = jnp.sum(jnp.where(matched, logits, 0.0), axis=1)
    row_max = lax.pmax(local_max, "vocab")
    shifted = jnp.exp(logits - row_max[:, None])
    totals, target_logit = lax.psum((jnp.sum(shifted, axis=1), local_target), "vocab")
    probs = shifted / totals[:, None]
    token_logp = target_logit - (row_max + jnp.log(totals))
    weights = response_mask.astype(jnp.float32)
    sequence_logp = jnp.sum((token_logp * weights).reshape(pair_local, 2, span), axis=2)
    ratios = sequence_logp - reference_sums
    margins = beta_scale * (ratios[:, 0] - ratios[:, 1])
    losses, slopes = pair_terms(margins, labels)
    mean_loss = lax.psum(jnp.sum(losses), "tok") / pair_total
    pair_coef = beta_scale * grad_scale / pair_total * slopes
    signed = jnp.stack([pair_coef, -pair_coef], axis=1)
    token_coef = (
        jnp.broadcast_to(signed[:, :, None], (pair_local, 2, span)).reshape(tok_rows) * weights
    )
    onehot = jnp.where(matched, 1.0, 0.0).astype(jnp.float32)
    dlogits = (token_coef[:, None] * (onehot - probs)).astype(jnp.bfloat16)
    dlogit_all = lax.all_gather(dlogits, "tok", axis=0, tiled=True)
    head_grad = lax.dot_general(
        token_cols, dlogit_all, (((0,), (0,)), ((), ())), preferred_element_type=jnp.float32
    ).astype(jnp.bfloat16)
    grad_cols = lax.psum_scatter(
        lax.dot_general(
            head_full, dlogits, (((1,), (1,)), ((), ())), preferred_element_type=jnp.float32
        ),
        "vocab",
        scatter_dimension=0,
        tiled=True,
    )
    hidden_grad = grad_cols.T.astype(jnp.bfloat16)
    return (mean_loss, margins, hidden_grad, head_grad)


def solution(mesh):
    return jax.shard_map(
        local,
        mesh=mesh,
        in_specs=(
            P("tok", "vocab"),
            P("tok", "vocab"),
            P("tok"),
            P("tok"),
            P("tok"),
            P("tok", None),
        ),
        out_specs=(P(), P("tok"), P("tok", "vocab"), P("tok", "vocab")),
        check_vma=False,
    )
```

profile of v0, /device:TPU:6, one launch (start us, length us, event | category | flops | bytes accessed | tf_op | source)
XLA Modules:
  0.0 756.5 jit_solution(17143302099194967058)
XLA Ops:
  7.2 0.0 all-gather.3.cloned.1.call-start
  7.2 0.7 all-gather.3.cloned.1.call-update
  7.9 0.0 all-gather.5.cloned.1.call-start
  8.6 116.4 %all_gather.9 = bf16[128,3584]{0,1:T(8,128)(2,1)} all-gather(bf16[128,56]{0,1:T(8,128)(2,1)} %param.6), channel_id=1, replica_groups=mesh['vocab'=64,'tok'=8] {'vocab'}, dimensions={1}, use_global_device_ids=true | all-gather | bytes 931840 | tf_op jit(solution)/shard_map/all_gather | solution.py:37
  125.0 5.4 fusion.10
  130.4 140.4 %pmax.7 = f32[128]{0:T(128)S(1)} all-reduce(f32[128]{0:T(128)S(1)} %get-tuple-element.22), channel_id=1, replica_groups=mesh['vocab'=64,'tok'=8] {'vocab'}, use_global_device_ids=true, to_apply=%region_3.4 | all-reduce | flops 128 | bytes 1024 | tf_op jit(solution)/shard_map/pmax | solution.py:46
  270.9 0.3 fusion.7
  271.2 138.0 %all-reduce.1 = (f32[128]{0:T(128)S(1)}, f32[128]{0:T(128)S(1)}) all-reduce(f32[128]{0:T(128)S(1)} %get-tuple-element.17, f32[128]{0:T(128)S(1)} %get-tuple-element.16), channel_id=1, replica_groups=mesh['vocab'=64,'tok'=8] {'vocab'}, use_global_device_ids=true, to_apply=%region_1.2 | all-reduce | flops 256 | bytes 2048 | tf_op jit(solution)/shard_map/psum | solution.py:48
  409.2 0.1 reshape.33
  409.2 0.1 reduce_sum.37
  409.4 0.6 fusion.9
  411.5 0.1 maximum_bitcast_fusion
  411.6 0.1 broadcast_in_dim.26
  411.7 0.1 broadcast_in_dim.27
  411.8 1.0 fusion.6
  412.8 4.8 all-to-all-start
  417.6 1.3 dynamic-slice
  419.8 19.0 %psum.23 = f32[]{:T(128)} all-reduce(f32[]{:T(128)} %bitcast.2), channel_id=1, replica_groups=mesh['vocab'=64,'tok'=8] {'tok'}, use_global_device_ids=true, to_apply=%region_7.8 | all-reduce | flops 1 | bytes 8 | tf_op jit(solution)/shard_map/psum | solution.py:56
  438.8 6.9 convolution_bitcast_fusion
  445.7 295.8 %all-reduce.3 = bf16[3584,128]{0,1:T(8,128)(2,1)S(1)} all-reduce(f32[3584,128]{0,1:T(8,128)S(1)} %convolution_bitcast_fusion), channel_id=2, replica_groups=mesh['vocab'=64,'tok'=8] {'vocab'}, use_global_device_ids=true, to_apply=%region_8.9.clone | all-reduce | flops 458752 | bytes 2752512
  741.5 0.1 fusion.8
  741.6 0.7 copy.14
  743.0 0.0 all-gather.5.cloned.1.call-done
  743.0 4.4 fusion
  (13 shorter events, 0.1 us)
Async XLA Ops:
  7.2 117.9 %all-gather.3.cloned.1.call-start = ((), (), s32[]{:S(2)}) async-start(), calls=%async_computation.1 | async-start | bytes 10321920 | tf_op jit(solution)/shard_map/all_gather | solution.py:39
  7.9 735.1 %all-gather.5.cloned.1.call-start = ((), (), s32[]{:S(2)}) async-start(), calls=%async_computation.2 | async-start | bytes 2949120 | tf_op jit(solution)/shard_map/all_gather | solution.py:64
  125.0 145.9 %copy-start = (s32[128]{0:T(128)S(1)}, s32[128]{0:T(128)}, u32[]{:S(2)}) copy-start(s32[128]{0:T(128)} %param.8) | copy-start | bytes 1540
  125.0 284.1 %copy-start.1 = (s32[128]{0:T(128)S(1)}, s32[128]{0:T(128)}, u32[]{:S(2)}) copy-start(s32[128]{0:T(128)} %param.9) | copy-start | bytes 1540
  125.0 284.4 %copy-start.2 = (f32[1,2]{1,0:T(1,128)S(1)}, f32[1,2]{1,0:T(1,128)}, u32[]{:S(2)}) copy-start(f32[1,2]{1,0:T(1,128)} %param.11) | copy-start | bytes 28
  412.8 330.2 %all-to-all-start = ((bf16[128,8,448]{0,2,1:T(8,128)(2,1)}), bf16[128,8,448]{0,2,1:T(8,128)(2,1)}, u32[]{:S(2)}, u32[]{:S(2)}) async-start(bf16[128,8,448]{0,2,1:T(8,128)(2,1)} %bitcast.8), calls=%async_computation | async-start | bytes 1835008 | tf_op jit(solution)/shard_map/all_to_all | solution.py:38
Sparse Core Ops, SparseCore 0:
  10.1 63.2 all-gather.2
  412.9 30.2 all-gather.4
where the time goes:
time: 757 us; the launch traced here: 756 us
  blocking collectives  710 us (94%)
  between operations  20.2 us (3%)
  matrix products  16.6 us (2%)
    unnamed x1, blocking collectives  296 us
    pmax x1, blocking collectives, local(): row_max = lax.pmax(local_max, 'vocab')  140 us
    psum x1, blocking collectives, local(): lax.psum((jnp.sum(shifted, axis=1), local_target), 'vocab')  138 us
    all_gather x1, blocking collectives, local(): rows_full = lax.all_gather(hidden, 'vocab', axis=1, tiled=True)  116 us
    psum x1, blocking collectives, local(): mean_loss = lax.psum(jnp.sum(losses), 'tok') / pair_total  19 us
  transfers between devices with their start and end apart: 3, of which 0 were waited for; matrix products, arithmetic and copies ran while one was open for 1% of the time, Pallas kernels for 0%

commit v1 on v0

v1 whole, which is shorter than its diff:
```python
import math

import jax
import jax.numpy as jnp
from jax import lax
from jax.experimental import pallas as pl
from jax.experimental.pallas import tpu as pltpu
from jax.sharding import PartitionSpec as P

MESH = pl.DeviceIdType.MESH

beta_scale = 0.1
tie_offset = math.log(2.0)
tie_const = math.log(3.0)
grad_scale = 512.0
pair_total = 8

Y, Z, T = 4, 16, 8
ROWS = 128
FEAT = 56
PAD = 64
DEPTH = 448
COLS = 1280
TILE = 256

f32 = jnp.float32
bf16 = jnp.bfloat16


def softplus(value):
    return jnp.maximum(value, 0.0) + jnp.log1p(jnp.exp(-jnp.abs(value)))


def sigmoid(value):
    return 1.0 / (1.0 + jnp.exp(-value))


def pair_terms(margins, winner):
    log_tie = (
        tie_const
        + margins
        - tie_offset
        - softplus(margins - tie_offset)
        - softplus(margins + tie_offset)
    )
    losses = winner * softplus(tie_offset - margins) - (1.0 - winner) * log_tie
    slopes = -winner * sigmoid(tie_offset - margins) - (1.0 - winner) * (
        1.0 - sigmoid(margins - tie_offset) - sigmoid(margins + tie_offset)
    )
    return losses, slopes


class TokGather:
    def __init__(self, own, buf, half, send, recv, v, t):
        self.own, self.buf, self.half, self.send, self.recv = own, buf, half, send, recv
        self.right = (v, lax.rem(t + 2, T))
        self.left = (v, lax.rem(t + 6, T))
        self.sib = (v, t + 1 - 2 * lax.rem(t, 2))
        self.t = t

    def copy(self, owner, part, slot, device, own=False):
        rows = pl.ds(part * self.half, self.half)
        dst = self.buf.at[owner, rows]
        return pltpu.make_async_remote_copy(
            src_ref=self.own.at[rows] if own else dst,
            dst_ref=dst,
            send_sem=self.send.at[slot],
            recv_sem=self.recv.at[owner, part],
            device_id=device,
            device_id_type=MESH,
        )

    def start(self):
        self.copy(self.t, 0, 0, self.right, True).start()
        self.copy(self.t, 1, 1, self.left, True).start()
        self.copy(self.t, 1, 2, self.right, True).start()
        self.copy(self.t, 0, 3, self.left, True).start()
        self.copy(self.t, 0, 4, self.sib, True).start()
        self.copy(self.t, 1, 5, self.sib, True).start()

    def wait(self, owner, part):
        self.copy(owner, part, 0, self.sib).wait_recv()

    def take(self, shift, part, slot):
        owner = lax.rem(self.t + shift, T)
        self.wait(owner, part)
        self.copy(owner, part, slot, self.sib).start()

    def first(self):
        behind, ahead = lax.rem(self.t + 6, T), lax.rem(self.t + 2, T)
        self.wait(behind, 0)
        self.copy(behind, 0, 6, self.right).start()
        self.copy(behind, 0, 8, self.sib).start()
        self.wait(ahead, 1)
        self.copy(ahead, 1, 7, self.left).start()
        self.copy(ahead, 1, 9, self.sib).start()

    def second(self):
        self.take(6, 1, 10)
        self.take(2, 0, 11)

    def third(self):
        self.take(4, 0, 12)
        self.take(4, 1, 13)

    def wait_sib(self, shift):
        owner = lax.rem(self.t + shift, T)
        owner = owner + 1 - 2 * lax.rem(owner, 2)
        self.wait(owner, 0)
        self.wait(owner, 1)

    def drain(self):
        for slot in range(14):
            self.copy(self.t, 0, slot, self.sib).wait_send()


def merge(stats, count):
    top = stats[0][0:1]
    for i in range(1, count):
        top = jnp.maximum(top, stats[i][0:1])
    total = jnp.zeros((1, ROWS), f32)
    target = jnp.zeros((1, ROWS), f32)
    for i in range(count):
        block = stats[i]
        total += block[1:2] * jnp.exp(block[0:1] - top)
        target += block[2:3]
    return top, total, target


def rows_of(block):
    return block.astype(f32)[:, :, :FEAT].reshape(DEPTH, ROWS)


def stack_rows(*parts):
    row = lax.broadcasted_iota(jnp.int32, (8, ROWS), 0)
    out = jnp.zeros((8, ROWS), f32)
    for i, part in enumerate(parts):
        out = jnp.where(row == i, part, out)
    return out


def kernel(
    hid, head, targets, mask, labels, refs,
    small, hg_out, head_grad,
    headbuf, hidbuf, hidt, logits, colbuf, lhs, dlog, rs_send, ybuf, zsend, zrecv,
    ystat, zstat, lossbuf,
    local_sem, head_send, head_recv, hz_send, hz_recv, hy_send, hy_recv, col_send, col_recv,
    sy_send, sy_recv, sz_send, sz_recv, dl_send, dl_recv, ry_send, ry_recv, rz_send, rz_recv,
    loss_send, loss_recv,
):
    v, t = lax.axis_index("vocab"), lax.axis_index("tok")
    z, y = lax.div(v, Y), lax.rem(v, Y)

    def at_y(k):
        return (z * Y + lax.rem(y + k, Y), t)

    def at_z(k):
        return (lax.rem(z + k, Z) * Y + y, t)

    def at_t(k):
        return (v, lax.rem(t + k, T))

    def remote(src, dst, send, recv, device):
        return pltpu.make_async_remote_copy(
            src_ref=src, dst_ref=dst, send_sem=send, recv_sem=recv,
            device_id=device, device_id_type=MESH,
        )

    own_head = pltpu.make_async_copy(head, headbuf.at[t], local_sem)
    own_head.start()

    barrier = pltpu.get_barrier_semaphore()
    for count, place in ((T, at_t), (Y, at_y), (Z, at_z)):
        for k in range(1, count):
            pl.semaphore_signal(barrier, inc=1, device_id=place(k), device_id_type=MESH)
    pl.semaphore_wait(barrier, T + Y + Z - 3)

    padded = jnp.concatenate([hid[...].astype(f32), jnp.zeros((PAD - FEAT, ROWS), f32)], axis=0)
    hidbuf[z, y] = padded.astype(bf16)

    def hid_z(k):
        mine = hidbuf.at[z, y]
        return remote(mine, mine, hz_send.at[k], hz_recv.at[k], at_z(k))

    for k in range(1, Z):
        hid_z(k).start()

    heads = TokGather(head, headbuf, DEPTH // 2, head_send, head_recv, v, t)
    heads.start()

    for k in range(1, Z):
        slot = hidbuf.at[lax.rem(z + Z - k, Z), y]
        remote(slot, slot, hz_send.at[k], hz_recv.at[k], at_z(k)).wait_recv()

    def hid_y(k, row):
        slot = hidbuf.at[:, row]
        return remote(slot, slot, hy_send.at[k], hy_recv.at[k], at_y(k))

    for k in range(1, Y):
        hid_y(k, y).start()
    heads.first()
    for k in range(1, Y):
        hid_y(k, lax.rem(y + Y - k, Y)).wait_recv()

    def turn(i, carry):
        hidt[i] = jnp.transpose(rows_of(hidbuf[pl.ds(2 * i, 2)])).astype(bf16)
        return carry

    lax.fori_loop(0, T, turn, 0)

    logits[...] = jnp.zeros_like(logits)

    def add_logits(shift, other):
        owner = lax.rem(t + shift, T)
        if other:
            owner = owner + 1 - 2 * lax.rem(owner, 2)

        def tile(j, carry):
            cols = pl.ds(pl.multiple_of(j * TILE, TILE), TILE)
            logits[:, cols] += jnp.dot(
                hidt[owner], headbuf[owner, :, cols], preferred_element_type=f32
            )
            return carry

        lax.fori_loop(0, COLS // TILE, tile, 0)

    own_head.wait()
    add_logits(0, False)
    heads.wait_sib(0)
    add_logits(0, True)
    heads.second()
    add_logits(6, False)
    add_logits(2, False)
    heads.wait_sib(6)
    add_logits(6, True)
    heads.wait_sib(2)
    add_logits(2, True)
    heads.third()
    add_logits(4, False)
    heads.wait_sib(4)
    add_logits(4, True)

    def col_copy(k):
        to = lax.rem(t + k, T)
        return remote(
            hidbuf.at[pl.ds(2 * to, 2)], colbuf.at[t], col_send.at[k], col_recv.at[k], at_t(k)
        )

    for k in range(1, T):
        col_copy(k).start()

    lane = lax.broadcasted_iota(jnp.int32, (ROWS, ROWS), 1)
    target_col = jnp.transpose(
        jnp.broadcast_to(targets[...].astype(f32), (ROWS, ROWS))
    )[:, 0:1].astype(jnp.int32)
    spot = target_col - v * COLS
    values = logits[...]
    column = lax.broadcasted_iota(jnp.int32, (ROWS, COLS), 1)
    local_max = jnp.max(values, axis=1, keepdims=True)
    local_target = jnp.sum(jnp.where(column == spot, values, 0.0), axis=1, keepdims=True)
    shifted = jnp.exp(values - local_max)
    logits[...] = shifted
    local_sum = jnp.sum(shifted, axis=1, keepdims=True)
    packed = jnp.where(lane == 0, local_max, jnp.where(lane == 1, local_sum, local_target))
    packed = jnp.transpose(packed)
    local_row = packed[0:1]
    ystat[0] = packed[0:8]

    def stat_y(k):
        return remote(ystat.at[0], ystat.at[k], sy_send.at[k], sy_recv.at[k], at_y(k))

    for k in range(1, Y):
        stat_y(k).start()
    for k in range(1, Y):
        stat_y(k).wait_recv()
    zstat[0] = stack_rows(*merge(ystat, Y))

    def stat_z(k):
        return remote(zstat.at[0], zstat.at[k], sz_send.at[k], sz_recv.at[k], at_z(k))

    for k in range(1, Z):
        stat_z(k).start()
    for k in range(1, Z):
        stat_z(k).wait_recv()
    row_max, totals, target_logit = merge(zstat, Z)

    token_logp = target_logit - (row_max + jnp.log(totals))
    weights = mask[...].astype(f32)
    scored = token_logp * weights
    chosen = lax.broadcasted_iota(jnp.int32, (1, ROWS), 1) < ROWS // 2
    sum_chosen = jnp.sum(jnp.where(chosen, scored, 0.0), axis=1, keepdims=True)
    sum_rejected = jnp.sum(jnp.where(chosen, 0.0, scored), axis=1, keepdims=True)
    margins = beta_scale * ((sum_chosen - refs[0, 0]) - (sum_rejected - refs[0, 1]))
    margins = jnp.broadcast_to(margins, (1, ROWS))
    losses, slopes = pair_terms(margins, labels[0].astype(f32))
    pair_coef = beta_scale * grad_scale / pair_total * slopes
    coef_row = jnp.where(chosen, pair_coef, -pair_coef) * weights
    scale_row = jnp.exp(local_row - row_max) / totals

    lossbuf[t] = jnp.broadcast_to(losses, (8, ROWS))

    def loss_copy(k):
        return remote(lossbuf.at[t], lossbuf.at[t], loss_send.at[k], loss_recv.at[k], at_t(k))

    for k in range(1, T):
        loss_copy(k).start()

    sub = lax.broadcasted_iota(jnp.int32, (ROWS, ROWS), 0)
    unpacked = jnp.transpose(jnp.where(sub == 0, coef_row, scale_row))
    coef, scale = unpacked[:, 0:1], unpacked[:, 1:2]
    onehot = jnp.where(column == spot, 1.0, 0.0)
    dlog[t] = (coef * (onehot - logits[...] * scale)).astype(bf16)

    grads = TokGather(dlog.at[t], dlog, ROWS // 2, dl_send, dl_recv, v, t)
    grads.start()

    first_pair = lax.div(z, 2)

    def part_y(p, k):
        return remote(
            rs_send.at[lax.rem(y + k, Y), pl.ds(2 * p, 2)],
            ybuf.at[k - 1, pl.ds(2 * p, 2)],
            ry_send.at[k - 1, p],
            ry_recv.at[k - 1, p],
            at_y(k),
        )

    def share(i, carry):
        p = lax.rem(first_pair + i, T)
        product = lax.dot_general(
            headbuf[p], dlog[t], (((1,), (1,)), ((), ())), preferred_element_type=f32
        ).reshape(2, Y, FEAT, ROWS)
        product = jnp.concatenate(
            [product, jnp.zeros((2, Y, PAD - FEAT, ROWS), f32)], axis=2
        ).astype(bf16)
        for row in range(Y):
            rs_send[row, pl.ds(2 * p, 2)] = product[:, row]
        for k in range(1, Y):
            part_y(p, k).start()
        return carry

    lax.fori_loop(0, T, share, 0)

    grads.first()

    def part_z(k):
        return remote(
            zsend.at[lax.rem(z + k, Z)], zrecv.at[k], rz_send.at[k], rz_recv.at[k], at_z(k)
        )

    def sum_y(i):
        p = lax.rem(first_pair + i, T)
        pair = pl.ds(2 * p, 2)
        for k in range(1, Y):
            part_y(p, k).wait_recv()
        total = rs_send[y, pair].astype(f32)
        for k in range(1, Y):
            total += ybuf[k - 1, pair].astype(f32)
        zsend[pair] = total.astype(bf16)
        return p

    sum_y(0)
    even = lax.rem(z, 2)
    part_z(lax.rem(Z + 1 - 2 * even, Z)).start()

    def pass_z(i, carry):
        p = sum_y(i)
        for j in range(2):
            part_z(lax.rem(2 * p + j + Z - z, Z)).start()
        return carry

    lax.fori_loop(1, T, pass_z, 0)

    grads.second()
    grads.third()

    for k in range(1, T):
        slot = colbuf.at[lax.rem(t + T - k, T)]
        remote(slot, slot, col_send.at[k], col_recv.at[k], at_t(k)).wait_recv()
    colbuf[t] = hidbuf[pl.ds(2 * t, 2)]

    def place(i, carry):
        lhs[:, pl.ds(pl.multiple_of(i * ROWS, ROWS), ROWS)] = rows_of(colbuf[i]).astype(bf16)
        return carry

    lax.fori_loop(0, T, place, 0)
    for shift in (0, 6, 2, 4):
        grads.wait_sib(shift)

    def head_tile(j, carry):
        cols = pl.ds(pl.multiple_of(j * TILE, TILE), TILE)
        rhs = dlog[:, :, cols].reshape(T * ROWS, TILE)
        head_grad[:, cols] = jnp.dot(lhs[...], rhs, preferred_element_type=f32).astype(bf16)
        return carry

    lax.fori_loop(0, COLS // TILE, head_tile, 0)

    total = zsend[z].astype(f32)
    for k in range(1, Z):
        part_z(k).wait_recv()
        total += zrecv[k].astype(f32)
    hg_out[...] = total[:FEAT].astype(bf16)

    for k in range(1, T):
        slot = lossbuf.at[lax.rem(t + T - k, T)]
        remote(slot, slot, loss_send.at[k], loss_recv.at[k], at_t(k)).wait_recv()
    mean_loss = jnp.zeros((1, ROWS), f32)
    for k in range(T):
        mean_loss += lossbuf[k][0:1]
    small[...] = stack_rows(mean_loss / pair_total, margins)

    heads.drain()
    grads.drain()
    for k in range(1, Z):
        hid_z(k).wait_send()
        stat_z(k).wait_send()
        part_z(k).wait_send()
    for k in range(1, Y):
        hid_y(k, y).wait_send()
        stat_y(k).wait_send()
    for k in range(1, T):
        col_copy(k).wait_send()
        loss_copy(k).wait_send()

    def drain_y(p, carry):
        for k in range(1, Y):
            part_y(p, k).wait_send()
        return carry

    lax.fori_loop(0, T, drain_y, 0)


def local(hidden, head_weight, targets, response_mask, labels, reference_sums):
    vmem = pl.BlockSpec(memory_space=pltpu.VMEM)
    smem = pl.BlockSpec(memory_space=pltpu.SMEM)
    dma = pltpu.SemaphoreType.DMA
    small, hg, head_grad = pl.pallas_call(
        kernel,
        out_shape=(
            jax.ShapeDtypeStruct((8, ROWS), f32),
            jax.ShapeDtypeStruct((FEAT, ROWS), bf16),
            jax.ShapeDtypeStruct((DEPTH, COLS), bf16),
        ),
        in_specs=[vmem, pl.BlockSpec(memory_space=pl.ANY), vmem, vmem, smem, smem],
        out_specs=(vmem, vmem, vmem),
        scratch_shapes=[
            pltpu.VMEM((T, DEPTH, COLS), bf16),
            pltpu.VMEM((Z, Y, PAD, ROWS), bf16),
            pltpu.VMEM((T, ROWS, DEPTH), bf16),
            pltpu.VMEM((ROWS, COLS), f32),
            pltpu.VMEM((T, 2, Y, PAD, ROWS), bf16),
            pltpu.VMEM((DEPTH, T * ROWS), bf16),
            pltpu.VMEM((T, ROWS, COLS), bf16),
            pltpu.VMEM((Y, Z, PAD, ROWS), bf16),
            pltpu.VMEM((Y - 1, Z, PAD, ROWS), bf16),
            pltpu.VMEM((Z, PAD, ROWS), bf16),
            pltpu.VMEM((Z, PAD, ROWS), bf16),
            pltpu.VMEM((Y, 8, ROWS), f32),
            pltpu.VMEM((Z, 8, ROWS), f32),
            pltpu.VMEM((T, 8, ROWS), f32),
            dma,
            dma((14,)),
            dma((T, 2)),
            dma((Z,)),
            dma((Z,)),
            dma((Y,)),
            dma((Y,)),
            dma((T,)),
            dma((T,)),
            dma((Y,)),
            dma((Y,)),
            dma((Z,)),
            dma((Z,)),
            dma((14,)),
            dma((T, 2)),
            dma((Y - 1, T)),
            dma((Y - 1, T)),
            dma((Z,)),
            dma((Z,)),
            dma((T,)),
            dma((T,)),
        ],
        compiler_params=pltpu.CompilerParams(
            collective_id=0, has_side_effects=True, vmem_limit_bytes=40 * 1024 * 1024
        ),
        cost_estimate=pl.CostEstimate(
            flops=6 * ROWS * DEPTH * T * COLS, bytes_accessed=4 * DEPTH * COLS, transcendentals=ROWS * COLS
        ),
    )(
        hidden.T,
        head_weight,
        targets.reshape(1, ROWS),
        response_mask.reshape(1, ROWS),
        labels,
        reference_sums,
    )
    return (small[0, 0], small[1, 0:1], hg.T, head_grad)


def solution(mesh):
    return jax.shard_map(
        local,
        mesh=mesh,
        in_specs=(
            P("tok", "vocab"),
            P("tok", "vocab"),
            P("tok"),
            P("tok"),
            P("tok"),
            P("tok", None),
        ),
        out_specs=(P(), P("tok"), P("tok", "vocab"), P("tok", "vocab")),
        check_vma=False,
    )
```

time: 757 us -> 105 us (0.14)
  the two profiles are of different devices: /device:TPU:6 before, /device:TPU:1 now
where the time goes in v1:
time: 105 us; the launch traced here: 104 us
  Pallas kernels  96.6 us (92%)
  local copies, waits for them, and re-layouts  6.05 us (6%)
  between operations  1.3 us (1%)
    pallas_call x1, Pallas kernels, local(): pl.pallas_call(kernel, out_shape=(jax.ShapeDtypeStruct((8, ROWS), f32), j...  96.6 us
    unnamed x12, local copies, waits for them, and re-layouts  5.53 us

profile of v1, /device:TPU:1, one launch (start us, length us, event | category | flops | bytes accessed | tf_op | source)
XLA Modules:
  0.0 104.0 jit_solution(9950765912729235664)
XLA Ops:
  1.3 0.0 copy-start
  1.3 1.2 %copy-done = bf16[448,1280]{1,0:T(8,128)(2,1)S(1)} copy-done((bf16[448,1280]{1,0:T(8,128)(2,1)S(1)}, bf16[448,1280]{1,0:T(8,128)(2,1)}, u32[]{:S(2)}) %copy-start) | copy-done | bytes 1146904
  2.5 0.0 copy-start.1
  2.5 0.7 copy-done.1
  3.3 0.0 copy-start.2
  3.3 0.7 copy-done.2
  3.9 0.0 copy-start.3
  3.9 0.7 copy-done.3
  4.6 0.0 copy-start.4
  4.6 0.7 copy-done.4
  5.2 96.6 %shard_map.93 = (f32[8,128]{1,0:T(8,128)S(1)}, bf16[56,128]{1,0:T(8,128)(2,1)S(1)}, bf16[448,1280]{1,0:T(8,128)(2,1)S(1)}) custom-call(bf16[56,128]{1,0:T(8,128)(2,1)S(1)} %bitcast.7, bf16[448,1280]{1,0:T(8,128)(2,1)S(1)} %copy-done, s32[1,128]{1,0:T(1,128)S(1)} %bitcast.8, s32[1,128]{1,0:T(1,128)S(1)} %bitcast.9, s32[1]{0:T(128)S(6)} %copy.12.labels, ...), custom_call_target="tpu_custom_call" | custom-call | flops 3523215360 | bytes 2293760 | tf_op jit(solution)/shard_map/pallas_call | solution.py:437
  101.8 0.5 fusion
  102.4 0.6 copy.13
  103.0 1.0 copy.14
Async XLA Ops:
  1.3 1.3 %copy-start = (bf16[448,1280]{1,0:T(8,128)(2,1)S(1)}, bf16[448,1280]{1,0:T(8,128)(2,1)}, u32[]{:S(2)}) copy-start(bf16[448,1280]{1,0:T(8,128)(2,1)} %head.1) | copy-start | bytes 3440644
  2.5 0.7 copy-start.1
  3.3 0.7 copy-start.2
  3.9 0.7 copy-start.3
  4.6 0.7 copy-start.4

commit v2 on v1

v2 whole, which is shorter than its diff:
```python
import math

import jax
import jax.numpy as jnp
from jax import lax
from jax.experimental import pallas as pl
from jax.experimental.pallas import tpu as pltpu
from jax.sharding import PartitionSpec as P

MESH = pl.DeviceIdType.MESH

beta_scale = 0.1
tie_offset = math.log(2.0)
tie_const = math.log(3.0)
grad_scale = 512.0
pair_total = 8

Y, Z, T = 4, 16, 8
ROWS = 128
FEAT = 56
PAD = 64
DEPTH = 448
COLS = 1280
TILE = 256

f32 = jnp.float32
bf16 = jnp.bfloat16


def softplus(value):
    return jnp.maximum(value, 0.0) + jnp.log1p(jnp.exp(-jnp.abs(value)))


def sigmoid(value):
    return 1.0 / (1.0 + jnp.exp(-value))


def pair_terms(margins, winner):
    log_tie = (
        tie_const
        + margins
        - tie_offset
        - softplus(margins - tie_offset)
        - softplus(margins + tie_offset)
    )
    losses = winner * softplus(tie_offset - margins) - (1.0 - winner) * log_tie
    slopes = -winner * sigmoid(tie_offset - margins) - (1.0 - winner) * (
        1.0 - sigmoid(margins - tie_offset) - sigmoid(margins + tie_offset)
    )
    return losses, slopes


class TokGather:
    def __init__(self, own, buf, half, send, recv, v, t):
        self.own, self.buf, self.half, self.send, self.recv = own, buf, half, send, recv
        self.right = (v, lax.rem(t + 2, T))
        self.left = (v, lax.rem(t + 6, T))
        self.sib = (v, t + 1 - 2 * lax.rem(t, 2))
        self.t = t

    def copy(self, owner, part, slot, device, own=False):
        rows = pl.ds(part * self.half, self.half)
        dst = self.buf.at[owner, rows]
        return pltpu.make_async_remote_copy(
            src_ref=self.own.at[rows] if own else dst,
            dst_ref=dst,
            send_sem=self.send.at[slot],
            recv_sem=self.recv.at[owner, part],
            device_id=device,
            device_id_type=MESH,
        )

    def start(self):
        self.copy(self.t, 0, 0, self.right, True).start()
        self.copy(self.t, 1, 1, self.left, True).start()
        self.copy(self.t, 1, 2, self.right, True).start()
        self.copy(self.t, 0, 3, self.left, True).start()
        self.copy(self.t, 0, 4, self.sib, True).start()
        self.copy(self.t, 1, 5, self.sib, True).start()

    def wait(self, owner, part):
        self.copy(owner, part, 0, self.sib).wait_recv()

    def take(self, shift, part, slot):
        owner = lax.rem(self.t + shift, T)
        self.wait(owner, part)
        self.copy(owner, part, slot, self.sib).start()

    def first(self):
        behind, ahead = lax.rem(self.t + 6, T), lax.rem(self.t + 2, T)
        self.wait(behind, 0)
        self.copy(behind, 0, 6, self.right).start()
        self.copy(behind, 0, 8, self.sib).start()
        self.wait(ahead, 1)
        self.copy(ahead, 1, 7, self.left).start()
        self.copy(ahead, 1, 9, self.sib).start()

    def second(self):
        self.take(6, 1, 10)
        self.take(2, 0, 11)

    def third(self):
        self.take(4, 0, 12)
        self.take(4, 1, 13)

    def wait_sib(self, shift):
        owner = lax.rem(self.t + shift, T)
        owner = owner + 1 - 2 * lax.rem(owner, 2)
        self.wait(owner, 0)
        self.wait(owner, 1)

    def drain(self):
        for slot in range(14):
            self.copy(self.t, 0, slot, self.sib).wait_send()


def merge(stats, count):
    top = stats[0][0:1]
    for i in range(1, count):
        top = jnp.maximum(top, stats[i][0:1])
    total = jnp.zeros((1, ROWS), f32)
    target = jnp.zeros((1, ROWS), f32)
    for i in range(count):
        block = stats[i]
        total += block[1:2] * jnp.exp(block[0:1] - top)
        target += block[2:3]
    return top, total, target


def pad_rows(block):
    return jnp.concatenate([block, jnp.zeros((PAD - FEAT, ROWS), f32)], axis=0).astype(bf16)


def stack_rows(*parts):
    row = lax.broadcasted_iota(jnp.int32, (8, ROWS), 0)
    out = jnp.zeros((8, ROWS), f32)
    for i, part in enumerate(parts):
        out = jnp.where(row == i, part, out)
    return out


def rows_of(buf, p):
    parts = [buf[row, p].astype(f32) for row in range(Y)]
    return jnp.concatenate(
        [parts[row][i * FEAT : (i + 1) * FEAT] for i in range(2) for row in range(Y)], axis=0
    )


def kernel(
    hid_in, head, targets_in, mask_in, labels_in, refs_in,
    small, hg_out, head_grad,
    hid, targets, mask, labels, refs,
    headbuf, hidz, colz, hidy, coly, hidt, logits, lhs, onehot, probs, dlog, chosen_rows,
    tsend, tybuf, tzsend, tzrecv, rsend, rybuf, rzsend, rzrecv, ystat, zstat, aux, names,
    in_sem, local_sem, head_send, head_recv, hz_send, hz_recv, hy_send, hy_recv,
    perm_send, perm_recv, cz_send, cz_recv, cy_send, cy_recv,
    sy_send, sy_recv, sz_send, sz_recv, pr_send, pr_recv,
    ty_send, ty_recv, tz_send, tz_recv, ry_send, ry_recv, rz_send, rz_recv,
    aux_send, aux_recv, name_send, name_recv, back_send, back_recv,
):
    v, t = lax.axis_index("vocab"), lax.axis_index("tok")
    z, y = lax.div(v, Y), lax.rem(v, Y)

    def at_y(k):
        return (z * Y + lax.rem(y + k, Y), t)

    def at_z(k):
        return (lax.rem(z + k, Z) * Y + y, t)

    def at_t(k):
        return (v, lax.rem(t + k, T))

    def remote(src, dst, send, recv, device):
        return pltpu.make_async_remote_copy(
            src_ref=src, dst_ref=dst, send_sem=send, recv_sem=recv,
            device_id=device, device_id_type=MESH,
        )

    own_head = pltpu.make_async_copy(head, headbuf.at[t], local_sem)
    own_head.start()
    inputs = [
        pltpu.make_async_copy(src, dst, in_sem.at[i])
        for i, (src, dst) in enumerate(
            (
                (hid_in, hid),
                (targets_in, targets),
                (mask_in, mask),
                (labels_in, labels),
                (refs_in, refs),
            )
        )
    ]
    for copy in inputs:
        copy.start()

    home = lax.div(z, 2)
    swap_z = 2 * t + lax.rem(z, 2)
    swap = (swap_z * Y + y, home)
    away = t != home

    barrier = pltpu.get_barrier_semaphore()
    for count, place in ((T, at_t), (Y, at_y), (Z, at_z)):
        for k in range(1, count):
            pl.semaphore_signal(barrier, inc=1, device_id=place(k), device_id_type=MESH)

    @pl.when(away)
    def _():
        pl.semaphore_signal(barrier, inc=1, device_id=swap, device_id_type=MESH)

    for copy in inputs:
        copy.wait()
    hidz[z] = pad_rows(hid[...].astype(f32))
    pl.semaphore_wait(barrier, T + Y + Z - 3 + away.astype(jnp.int32))

    def spread_z(buf, send, recv, k):
        return remote(buf.at[z], buf.at[z], send.at[k], recv.at[k], at_z(k))

    def await_z(buf, send, recv):
        for k in range(1, Z):
            slot = buf.at[lax.rem(z + Z - k, Z)]
            remote(slot, slot, send.at[k], recv.at[k], at_z(k)).wait_recv()

    def spread_y(buf, send, recv, k):
        return remote(buf.at[y], buf.at[y], send.at[k], recv.at[k], at_y(k))

    def await_y(buf, send, recv):
        for k in range(1, Y):
            slot = buf.at[lax.rem(y + Y - k, Y)]
            remote(slot, slot, send.at[k], recv.at[k], at_y(k)).wait_recv()

    def repack(src, dst):
        def pair(p, carry):
            both = [src[2 * p + i].astype(f32)[:FEAT] for i in range(2)]
            dst[y, p] = jnp.concatenate(both, axis=0).astype(bf16)
            return carry

        lax.fori_loop(0, T, pair, 0)

    names[t] = jnp.broadcast_to(targets[...].astype(f32), (8, ROWS))

    def name_copy(k):
        return remote(names.at[t], names.at[t], name_send.at[k], name_recv.at[k], at_t(k))

    for k in range(1, T):
        name_copy(k).start()
    swap_copy = remote(hidz.at[z], colz.at[swap_z], perm_send, perm_recv, swap)
    pl.when(away)(swap_copy.start)
    for k in range(1, Z):
        spread_z(hidz, hz_send, hz_recv, k).start()

    heads = TokGather(head, headbuf, DEPTH // 2, head_send, head_recv, v, t)
    heads.start()

    @pl.when(jnp.logical_not(away))
    def _():
        colz[z] = pad_rows(hid[...].astype(f32))

    lane = lax.broadcasted_iota(jnp.int32, (ROWS, ROWS), 1)
    column = lax.broadcasted_iota(jnp.int32, (ROWS, COLS), 1)

    def spot_of(owner):
        wide = jnp.concatenate([names[owner]] * (ROWS // 8), axis=0)
        return jnp.transpose(wide)[:, 0:1].astype(jnp.int32) - v * COLS

    spot = spot_of(t)
    logits[...] = jnp.zeros_like(logits)

    def owner_of(shift, other):
        owner = lax.rem(t + shift, T)
        if other:
            owner = owner + 1 - 2 * lax.rem(owner, 2)
        return owner

    def share(rows, matrix, send, p, part):
        product = lax.dot_general(
            headbuf[rows], matrix, (((1,), (1,)), ((), ())), preferred_element_type=f32
        ).reshape(2, Y, FEAT, ROWS)
        for row in range(Y):
            send[row, p] = product[:, row].reshape(2 * FEAT, ROWS).astype(bf16)
        for k in range(1, Y):
            part(p, k).start()

    def sum_y(send, recv, out, p, part, factors):
        for k in range(1, Y):
            part(p, k).wait_recv()
        total = send[y, p].astype(f32)
        if factors is not None:
            total = total * factors[0]
        for k in range(1, Y):
            term = recv[k - 1, p].astype(f32)
            total += term if factors is None else term * factors[k]
        out[2 * p] = pad_rows(total[:FEAT])
        out[2 * p + 1] = pad_rows(total[FEAT:])

    def target_y(p, k):
        return remote(
            tsend.at[lax.rem(y + k, Y), p], tybuf.at[k - 1, p],
            ty_send.at[k - 1, p], ty_recv.at[k - 1, p], at_y(k),
        )

    def target_z(k):
        return remote(
            tzsend.at[lax.rem(z + k, Z)], tzrecv.at[k], tz_send.at[k], tz_recv.at[k], at_z(k)
        )

    own_head.wait()
    for k in range(1, T):
        slot = names.at[lax.rem(t + T - k, T)]
        remote(slot, slot, name_send.at[k], name_recv.at[k], at_t(k)).wait_recv()

    def target_share(i, carry):
        onehot[...] = jnp.where(column == spot_of(i), 1.0, 0.0).astype(bf16)
        share(t, onehot[...], tsend, i, target_y)
        return carry

    lax.fori_loop(0, T, target_share, 0)

    await_z(hidz, hz_send, hz_recv)
    repack(hidz, hidy)
    for k in range(1, Y):
        spread_y(hidy, hy_send, hy_recv, k).start()
    pl.when(away)(swap_copy.wait)
    for k in range(1, Z):
        spread_z(colz, cz_send, cz_recv, k).start()
    heads.first()
    await_y(hidy, hy_send, hy_recv)

    def turn(i, carry):
        hidt[i] = jnp.transpose(rows_of(hidy, i)).astype(bf16)
        return carry

    lax.fori_loop(0, T, turn, 0)

    def add_logits(shift, other):
        owner = owner_of(shift, other)

        def tile(j, carry):
            cols = pl.ds(pl.multiple_of(j * TILE, TILE), TILE)
            logits[:, cols] += jnp.dot(
                hidt[owner], headbuf[owner, :, cols], preferred_element_type=f32
            )
            return carry

        lax.fori_loop(0, COLS // TILE, tile, 0)

    add_logits(0, False)
    heads.wait_sib(0)
    add_logits(0, True)

    await_z(colz, cz_send, cz_recv)
    repack(colz, coly)
    for k in range(1, Y):
        spread_y(coly, cy_send, cy_recv, k).start()

    def target_pass(i, carry):
        sum_y(tsend, tybuf, tzsend, i, target_y, None)
        return carry

    lax.fori_loop(0, T, target_pass, 0)
    for k in range(1, Z):
        target_z(k).start()

    heads.second()
    add_logits(6, False)
    add_logits(2, False)
    heads.wait_sib(6)
    add_logits(6, True)
    heads.wait_sib(2)
    add_logits(2, True)
    heads.third()
    add_logits(4, False)
    heads.wait_sib(4)
    add_logits(4, True)

    values = logits[...]
    hit = column == spot
    local_max = jnp.max(values, axis=1, keepdims=True)
    shifted = jnp.exp(values - local_max)
    probs[t] = jnp.where(hit, 0.0, shifted).astype(bf16)
    grads = TokGather(probs.at[t], probs, ROWS // 2, pr_send, pr_recv, v, t)
    local_target = jnp.sum(jnp.where(hit, values, 0.0), axis=1, keepdims=True)
    local_sum = jnp.sum(shifted, axis=1, keepdims=True)
    packed = jnp.where(lane == 0, local_max, jnp.where(lane == 1, local_sum, local_target))
    packed = jnp.transpose(packed)
    local_row = packed[0:1]
    ystat[0] = packed[0:8]

    def stat_y(k):
        return remote(ystat.at[0], ystat.at[k], sy_send.at[k], sy_recv.at[k], at_y(k))

    for k in range(1, Y):
        stat_y(k).start()
    grads.start()

    def pair_at(i):
        far = T // 2 + lax.div(i + 1, 2) * (1 - 2 * lax.rem(i, 2))
        return lax.rem(home + far, T)

    def part_y(p, k):
        return remote(
            rsend.at[lax.rem(y + k, Y), p], rybuf.at[k - 1, p],
            ry_send.at[k - 1, p], ry_recv.at[k - 1, p], at_y(k),
        )

    def part_z(k):
        return remote(
            rzsend.at[lax.rem(z + k, Z)], rzrecv.at[k], rz_send.at[k], rz_recv.at[k], at_z(k)
        )

    def raw_share(i):
        p = pair_at(i)
        share(p, probs[t], rsend, p, part_y)

    raw_share(jnp.int32(0))

    for k in range(1, Y):
        stat_y(k).wait_recv()
    y_stats = merge(ystat, Y)
    zstat[0] = stack_rows(*y_stats)

    def stat_z(k):
        return remote(zstat.at[0], zstat.at[k], sz_send.at[k], sz_recv.at[k], at_z(k))

    for k in range(1, Z):
        stat_z(k).start()
    factors = [jnp.exp(ystat[k][0:1] - y_stats[0]) for k in range(Y)]

    def raw_pass(i):
        p = pair_at(i)
        sum_y(rsend, rybuf, rzsend, p, part_y, factors)
        for j in range(2):
            k = lax.rem(2 * p + j + Z - z, Z)

            @pl.when(k != 0)
            def _():
                part_z(k).start()

    def both(i, carry):
        raw_share(i)
        raw_pass(i - 3)
        return carry

    raw_share(jnp.int32(1))
    raw_share(jnp.int32(2))
    lax.fori_loop(3, 5, both, 0)
    grads.first()
    lax.fori_loop(5, T, both, 0)
    grads.second()

    found = tzsend[z].astype(f32)
    for k in range(1, Z):
        target_z(k).wait_recv()
        found += tzrecv[k].astype(f32)
    tzrecv[0] = found.astype(bf16)
    back_copy = remote(tzrecv.at[0], chosen_rows, back_send, back_recv, swap)
    pl.when(away)(back_copy.start)

    @pl.when(jnp.logical_not(away))
    def _():
        chosen_rows[...] = tzrecv[0]

    await_y(coly, cy_send, cy_recv)

    for i in range(T):
        lhs[:, i * ROWS : (i + 1) * ROWS] = rows_of(coly, i).astype(bf16)

    for k in range(1, Z):
        stat_z(k).wait_recv()
    row_max, totals, target_logit = merge(zstat, Z)
    token_logp = target_logit - (row_max + jnp.log(totals))
    weights = mask[...].astype(f32)
    scored = token_logp * weights
    chosen = lax.broadcasted_iota(jnp.int32, (1, ROWS), 1) < ROWS // 2
    sum_chosen = jnp.sum(jnp.where(chosen, scored, 0.0), axis=1, keepdims=True)
    sum_rejected = jnp.sum(jnp.where(chosen, 0.0, scored), axis=1, keepdims=True)
    margins = beta_scale * ((sum_chosen - refs[0, 0]) - (sum_rejected - refs[0, 1]))
    margins = jnp.broadcast_to(margins, (1, ROWS))
    losses, slopes = pair_terms(margins, labels[0].astype(f32))
    pair_coef = beta_scale * grad_scale / pair_total * slopes
    coef = jnp.where(chosen, pair_coef, -pair_coef) * weights
    target_coef = coef * (1.0 - jnp.exp(target_logit - row_max) / totals)
    scale = coef * jnp.exp(local_row - row_max) / totals
    aux[t] = stack_rows(scale, target_coef, losses)

    def aux_copy(k):
        return remote(aux.at[t], aux.at[t], aux_send.at[k], aux_recv.at[k], at_t(k))

    for k in range(1, T):
        aux_copy(k).start()

    lax.fori_loop(T - 3, T, lambda i, carry: (raw_pass(i), carry)[1], 0)
    grads.third()
    for k in range(1, T):
        slot = aux.at[lax.rem(t + T - k, T)]
        remote(slot, slot, aux_send.at[k], aux_recv.at[k], at_t(k)).wait_recv()

    for shift in (0, 6, 2, 4):
        grads.wait_sib(shift)

    def block(owner, carry):
        rows = jnp.transpose(jnp.concatenate([aux[owner]] * (ROWS // 8), axis=0))
        dlog[owner] = jnp.where(
            column == spot_of(owner), rows[:, 1:2], -rows[:, 0:1] * probs[owner].astype(f32)
        ).astype(bf16)
        return carry

    lax.fori_loop(0, T, block, 0)

    def head_tile(j, carry):
        cols = pl.ds(pl.multiple_of(j * TILE, TILE), TILE)
        rhs = dlog[:, :, cols].reshape(T * ROWS, TILE)
        head_grad[:, cols] = jnp.dot(lhs[...], rhs, preferred_element_type=f32).astype(bf16)
        return carry

    lax.fori_loop(0, COLS // TILE, head_tile, 0)

    pl.when(away)(back_copy.wait)
    chosen_columns = chosen_rows[...].astype(f32)
    others = rzsend[z].astype(f32) * jnp.exp(zstat[0][0:1] - row_max)
    for k in range(1, Z):
        part_z(k).wait_recv()
        others += rzrecv[k].astype(f32) * jnp.exp(zstat[k][0:1] - row_max)
    grad = target_coef * chosen_columns - (coef / totals) * others
    hg_out[...] = grad[:FEAT].astype(bf16)

    mean_loss = jnp.zeros((1, ROWS), f32)
    for k in range(T):
        mean_loss += aux[k][2:3]
    small[...] = stack_rows(mean_loss / pair_total, margins)

    heads.drain()
    grads.drain()
    for k in range(1, Z):
        spread_z(hidz, hz_send, hz_recv, k).wait_send()
        spread_z(colz, cz_send, cz_recv, k).wait_send()
        stat_z(k).wait_send()
        target_z(k).wait_send()
        part_z(k).wait_send()
    for k in range(1, Y):
        spread_y(hidy, hy_send, hy_recv, k).wait_send()
        spread_y(coly, cy_send, cy_recv, k).wait_send()
        stat_y(k).wait_send()
    for k in range(1, T):
        aux_copy(k).wait_send()
        name_copy(k).wait_send()

    def drain_y(p, carry):
        for k in range(1, Y):
            target_y(p, k).wait_send()
            part_y(p, k).wait_send()
        return carry

    lax.fori_loop(0, T, drain_y, 0)


def local(hidden, head_weight, targets, response_mask, labels, reference_sums):
    vmem = pl.BlockSpec(memory_space=pltpu.VMEM)
    dma = pltpu.SemaphoreType.DMA
    small, hg, head_grad = pl.pallas_call(
        kernel,
        out_shape=(
            jax.ShapeDtypeStruct((8, ROWS), f32),
            jax.ShapeDtypeStruct((FEAT, ROWS), bf16),
            jax.ShapeDtypeStruct((DEPTH, COLS), bf16),
        ),
        in_specs=[pl.BlockSpec(memory_space=pl.ANY)] * 6,
        out_specs=(vmem, vmem, vmem),
        scratch_shapes=[
            pltpu.VMEM((FEAT, ROWS), bf16),
            pltpu.VMEM((1, ROWS), jnp.int32),
            pltpu.VMEM((1, ROWS), jnp.int32),
            pltpu.SMEM((1,), jnp.int32),
            pltpu.SMEM((1, 2), f32),
            pltpu.VMEM((T, DEPTH, COLS), bf16),
            pltpu.VMEM((Z, PAD, ROWS), bf16),
            pltpu.VMEM((Z, PAD, ROWS), bf16),
            pltpu.VMEM((Y, T, 2 * FEAT, ROWS), bf16),
            pltpu.VMEM((Y, T, 2 * FEAT, ROWS), bf16),
            pltpu.VMEM((T, ROWS, DEPTH), bf16),
            pltpu.VMEM((ROWS, COLS), f32),
            pltpu.VMEM((DEPTH, T * ROWS), bf16),
            pltpu.VMEM((ROWS, COLS), bf16),
            pltpu.VMEM((T, ROWS, COLS), bf16),
            pltpu.VMEM((T, ROWS, COLS), bf16),
            pltpu.VMEM((PAD, ROWS), bf16),
        ]
        + [
            pltpu.VMEM((Y, T, 2 * FEAT, ROWS), bf16),
            pltpu.VMEM((Y - 1, T, 2 * FEAT, ROWS), bf16),
            pltpu.VMEM((Z, PAD, ROWS), bf16),
            pltpu.VMEM((Z, PAD, ROWS), bf16),
        ]
        * 2
        + [
            pltpu.VMEM((Y, 8, ROWS), f32),
            pltpu.VMEM((Z, 8, ROWS), f32),
            pltpu.VMEM((T, 8, ROWS), f32),
            pltpu.VMEM((T, 8, ROWS), f32),
            dma((5,)),
            dma,
            dma((14,)),
            dma((T, 2)),
        ]
        + [dma((Z,)), dma((Z,)), dma((Y,)), dma((Y,))]
        + [dma, dma]
        + [dma((Z,)), dma((Z,)), dma((Y,)), dma((Y,))]
        + [dma((Y,)), dma((Y,)), dma((Z,)), dma((Z,))]
        + [dma((14,)), dma((T, 2))]
        + [dma((Y - 1, T)), dma((Y - 1, T)), dma((Z,)), dma((Z,))] * 2
        + [dma((T,)), dma((T,))] * 2
        + [dma, dma],
        compiler_params=pltpu.CompilerParams(
            collective_id=0, has_side_effects=True, vmem_limit_bytes=40 * 1024 * 1024
        ),
        cost_estimate=pl.CostEstimate(
            flops=6 * ROWS * DEPTH * T * COLS, bytes_accessed=4 * DEPTH * COLS, transcendentals=ROWS * COLS
        ),
    )(
        hidden.T,
        head_weight,
        targets.reshape(1, ROWS),
        response_mask.reshape(1, ROWS),
        labels,
        reference_sums,
    )
    return (small[0, 0], small[1, 0:1], hg.T, head_grad)


def solution(mesh):
    return jax.shard_map(
        local,
        mesh=mesh,
        in_specs=(
            P("tok", "vocab"),
            P("tok", "vocab"),
            P("tok"),
            P("tok"),
            P("tok"),
            P("tok", None),
        ),
        out_specs=(P(), P("tok"), P("tok", "vocab"), P("tok", "vocab")),
        check_vma=False,
    )
```

time: 105 us -> 94.7 us (0.902)
  Pallas kernels: 96.6 us -> 86.2 us
    pallas_call x1, Pallas kernels: 96.6 us -> 86.2 us  [local(): pl.pallas_call(kernel, out_shape=(jax.ShapeDtypeStruct((8, ROWS), f32), j...]
where the time goes in v2:
time: 94.7 us; the launch traced here: 93.6 us
  Pallas kernels  86.2 us (91%)
  local copies, waits for them, and re-layouts  6.05 us (6%)
  between operations  1.3 us (1%)
    pallas_call x1, Pallas kernels, local(): pl.pallas_call(kernel, out_shape=(jax.ShapeDtypeStruct((8, ROWS), f32), j...  86.2 us
    unnamed x12, local copies, waits for them, and re-layouts  5.53 us

profile of v2, /device:TPU:1, one launch (start us, length us, event | category | flops | bytes accessed | tf_op | source)
XLA Modules:
  0.0 93.6 jit_solution(4159038112277662587)
XLA Ops:
  1.3 0.0 copy-start
  1.3 1.2 %copy-done = bf16[448,1280]{1,0:T(8,128)(2,1)S(1)} copy-done((bf16[448,1280]{1,0:T(8,128)(2,1)S(1)}, bf16[448,1280]{1,0:T(8,128)(2,1)}, u32[]{:S(2)}) %copy-start) | copy-done | bytes 1146904
  2.5 0.0 copy-start.1
  2.5 0.7 copy-done.1
  3.3 0.0 copy-start.2
  3.3 0.7 copy-done.2
  3.9 0.0 copy-start.3
  3.9 0.7 copy-done.3
  4.6 0.0 copy-start.4
  4.6 0.7 copy-done.4
  5.2 86.2 %shard_map.93 = (f32[8,128]{1,0:T(8,128)S(1)}, bf16[56,128]{1,0:T(8,128)(2,1)S(1)}, bf16[448,1280]{1,0:T(8,128)(2,1)S(1)}) custom-call(bf16[56,128]{1,0:T(8,128)(2,1)S(1)} %bitcast.7, bf16[448,1280]{1,0:T(8,128)(2,1)S(1)} %copy-done, s32[1,128]{1,0:T(1,128)S(1)} %bitcast.8, s32[1,128]{1,0:T(1,128)S(1)} %bitcast.9, s32[1]{0:T(128)S(6)} %copy.12.labels_in, ...), custom_call_target="tpu_custom_call" | custom-call | flops 3523215360 | bytes 2293760 | tf_op jit(solution)/shard_map/pallas_call | solution.py:559
  91.5 0.5 fusion
  92.0 0.6 copy.13
  92.6 1.0 %copy.14 = bf16[448,1280]{1,0:T(8,128)(2,1)} copy(bf16[448,1280]{1,0:T(8,128)(2,1)S(1)} %get-tuple-element.19) | data formatting | bytes 2293760
Async XLA Ops:
  1.3 1.3 %copy-start = (bf16[448,1280]{1,0:T(8,128)(2,1)S(1)}, bf16[448,1280]{1,0:T(8,128)(2,1)}, u32[]{:S(2)}) copy-start(bf16[448,1280]{1,0:T(8,128)(2,1)} %head.1) | copy-start | bytes 3440644
  2.5 0.7 copy-start.1
  3.3 0.7 copy-start.2
  3.9 0.7 copy-start.3
  4.6 0.7 copy-start.4

commit v3 on v2

--- a/solution.py
+++ b/solution.py
@@ -277,7 +277,7 @@
         ).reshape(2, Y, FEAT, ROWS)
         for row in range(Y):
             send[row, p] = product[:, row].reshape(2 * FEAT, ROWS).astype(bf16)
-        for k in range(1, Y):
+        for k in (2, 1, 3):
             part(p, k).start()
 
     def sum_y(send, recv, out, p, part, factors):
@@ -390,7 +390,6 @@
 
     for k in range(1, Y):
         stat_y(k).start()
-    grads.start()
 
     def pair_at(i):
         far = T // 2 + lax.div(i + 1, 2) * (1 - 2 * lax.rem(i, 2))
@@ -412,6 +411,7 @@
         share(p, probs[t], rsend, p, part_y)
 
     raw_share(jnp.int32(0))
+    grads.start()
 
     for k in range(1, Y):
         stat_y(k).wait_recv()
@@ -435,17 +435,9 @@
             def _():
                 part_z(k).start()
 
-    def both(i, carry):
-        raw_share(i)
-        raw_pass(i - 3)
-        return carry
-
-    raw_share(jnp.int32(1))
-    raw_share(jnp.int32(2))
-    lax.fori_loop(3, 5, both, 0)
+    lax.fori_loop(1, T, lambda i, carry: (raw_share(i), carry)[1], 0)
     grads.first()
-    lax.fori_loop(5, T, both, 0)
-    grads.second()
+    lax.fori_loop(0, 3, lambda i, carry: (raw_pass(i), carry)[1], 0)
 
     found = tzsend[z].astype(f32)
     for k in range(1, Z):
@@ -488,14 +480,11 @@
     for k in range(1, T):
         aux_copy(k).start()
 
-    lax.fori_loop(T - 3, T, lambda i, carry: (raw_pass(i), carry)[1], 0)
-    grads.third()
+    grads.second()
+    lax.fori_loop(3, T, lambda i, carry: (raw_pass(i), carry)[1], 0)
     for k in range(1, T):
         slot = aux.at[lax.rem(t + T - k, T)]
         remote(slot, slot, aux_send.at[k], aux_recv.at[k], at_t(k)).wait_recv()
-
-    for shift in (0, 6, 2, 4):
-        grads.wait_sib(shift)
 
     def block(owner, carry):
         rows = jnp.transpose(jnp.concatenate([aux[owner]] * (ROWS // 8), axis=0))
@@ -504,7 +493,15 @@
         ).astype(bf16)
         return carry
 
-    lax.fori_loop(0, T, block, 0)
+    def chip_rows(shift):
+        grads.wait_sib(shift)
+        chip = lax.div(lax.rem(t + shift, T), 2)
+        lax.fori_loop(2 * chip, 2 * chip + 2, block, 0)
+
+    chip_rows(0)
+    grads.third()
+    for shift in (6, 2, 4):
+        chip_rows(shift)
 
     def head_tile(j, carry):
         cols = pl.ds(pl.multiple_of(j * TILE, TILE), TILE)

time: 94.7 us -> 94.3 us (level)
  no operation moved by 1% of the time
where the time goes in v3:
time: 94.3 us; the launch traced here: 94.1 us
  Pallas kernels  86.7 us (92%)
  local copies, waits for them, and re-layouts  6.05 us (6%)
  between operations  1.3 us (1%)
    pallas_call x1, Pallas kernels, local(): pl.pallas_call(kernel, out_shape=(jax.ShapeDtypeStruct((8, ROWS), f32), j...  86.7 us
    unnamed x12, local copies, waits for them, and re-layouts  5.53 us

profile of v3, /device:TPU:1, one launch (start us, length us, event | category | flops | bytes accessed | tf_op | source)
XLA Modules:
  0.0 94.1 jit_solution(13271766578610687516)
XLA Ops:
  1.3 0.0 copy-start
  1.3 1.2 %copy-done = bf16[448,1280]{1,0:T(8,128)(2,1)S(1)} copy-done((bf16[448,1280]{1,0:T(8,128)(2,1)S(1)}, bf16[448,1280]{1,0:T(8,128)(2,1)}, u32[]{:S(2)}) %copy-start) | copy-done | bytes 1146904
  2.5 0.0 copy-start.1
  2.5 0.7 copy-done.1
  3.3 0.0 copy-start.2
  3.3 0.7 copy-done.2
  3.9 0.0 copy-start.3
  3.9 0.7 copy-done.3
  4.6 0.0 copy-start.4
  4.6 0.7 copy-done.4
  5.2 86.7 %shard_map.93 = (f32[8,128]{1,0:T(8,128)S(1)}, bf16[56,128]{1,0:T(8,128)(2,1)S(1)}, bf16[448,1280]{1,0:T(8,128)(2,1)S(1)}) custom-call(bf16[56,128]{1,0:T(8,128)(2,1)S(1)} %bitcast.7, bf16[448,1280]{1,0:T(8,128)(2,1)S(1)} %copy-done, s32[1,128]{1,0:T(1,128)S(1)} %bitcast.8, s32[1,128]{1,0:T(1,128)S(1)} %bitcast.9, s32[1]{0:T(128)S(6)} %copy.12.labels_in, ...), custom_call_target="tpu_custom_call" | custom-call | flops 3523215360 | bytes 2293760 | tf_op jit(solution)/shard_map/pallas_call | solution.py:556
  91.9 0.5 fusion
  92.5 0.6 copy.13
  93.1 1.0 %copy.14 = bf16[448,1280]{1,0:T(8,128)(2,1)} copy(bf16[448,1280]{1,0:T(8,128)(2,1)S(1)} %get-tuple-element.19) | data formatting | bytes 2293760
Async XLA Ops:
  1.3 1.3 %copy-start = (bf16[448,1280]{1,0:T(8,128)(2,1)S(1)}, bf16[448,1280]{1,0:T(8,128)(2,1)}, u32[]{:S(2)}) copy-start(bf16[448,1280]{1,0:T(8,128)(2,1)} %head.1) | copy-start | bytes 3440644
  2.5 0.7 copy-start.1
  3.3 0.7 copy-start.2
  3.9 0.7 copy-start.3
  4.6 0.7 copy-start.4
